TPU v7x, 32 devices: a whole 2x2x4 slice. The times are simulated.
32 devices in a mesh: depth: 4 (over y, x), res: 8 (over z, core).
Axes of the slice: x: 2, y: 2, z: 4, core: 2. Of those that a mesh axis runs over, the one named last changes fastest.
Arguments:
- family_activity: bfloat16 [1024, 8, 768], P('depth', 'res'), may hold values from -6 to 6
- rescale_factor: float32 [768], replicated, may hold values from 0.25 to 1.75
- asking_weights: bfloat16 [768, 768], P(('depth', 'res')), may hold values from -1.203125 to 1.203125
- lookup_weights: bfloat16 [768, 768], P(('depth', 'res')), may hold values from -1.203125 to 1.203125
- payload_weights: bfloat16 [768, 768], P(('depth', 'res')), may hold values from -0.21875 to 0.21875
- exit_weights: bfloat16 [768, 768], P(('depth', 'res')), may hold values from -0.625 to 0.625
- upstream_adjoint: bfloat16 [1024, 8, 768], P('depth', 'res'), may hold values from -6 to 6
Outputs:
- final_result: bfloat16 [1024, 8, 768], P('depth', 'res')
- alignment_gradient: bfloat16 [1024, 8, 768], P('depth', 'res')
- query_gradient: float32 [768, 768], P(('depth', 'res'))
- key_gradient: float32 [768, 768], P(('depth', 'res'))
- value_gradient: float32 [768, 768], P(('depth', 'res'))
- output_gradient: float32 [768, 768], P(('depth', 'res'))
- gain_gradient: float32 [768], P(('depth', 'res'))
All inputs are finite; a program needn't handle non-finite values.
Results may differ from a plain program's by a relative error of at most 0.022.
The roundings to bfloat16 on the way count: a program that leaves them out, or rounds other values in their place, can miss the bound.
Values may be sent and summed in bfloat16 or wider, within the bound.
No kernel may reach another device: no remote copies, remote signals or barrier semaphores. Data moves between devices by JAX's collectives and lax.ppermute only.
A program may use at most 128 MiB of HBM per device.

v0:
```python
import jax
import jax.numpy as jnp
from jax import lax
from jax.sharding import PartitionSpec as P

HEADS = 12
HEAD_DIM = 64


def standardize_entries(family_activity, rescale_factor):
    payload_entries = family_activity.astype(jnp.float32)
    centered = payload_entries - jnp.mean(payload_entries, axis=-1, keepdims=True)
    reciprocal_spread = lax.rsqrt(jnp.mean(centered * centered, axis=-1, keepdims=True) + 1e-05)
    standardized_entries = centered * reciprocal_spread
    return (
        (standardized_entries * rescale_factor).astype(jnp.bfloat16),
        standardized_entries,
        reciprocal_spread,
    )


def project(rows, weight, factor):
    return (factor * jnp.dot(rows, weight, preferred_element_type=jnp.float32)).astype(jnp.bfloat16)


def to_heads(array):
    count, cols = (array.shape[0], array.shape[1])
    return jnp.transpose(array.reshape(count, cols, HEADS, HEAD_DIM), (1, 2, 0, 3)).reshape(
        cols * HEADS, count, HEAD_DIM
    )


def from_heads(array, cols):
    count = array.shape[1]
    return jnp.transpose(array.reshape(cols, HEADS, count, HEAD_DIM), (2, 0, 1, 3)).reshape(
        count, cols, HEADS * HEAD_DIM
    )


def head_pass(query, keys, payload_entries, d_att):
    scale = HEAD_DIM ** (-0.5)
    scores = jnp.dot(query, keys.T, preferred_element_type=jnp.float32)
    probs = jax.nn.softmax(scores, axis=-1)
    probs_b = probs.astype(jnp.bfloat16)
    mixed_homologs = jnp.dot(probs_b, payload_entries, preferred_element_type=jnp.float32).astype(
        jnp.bfloat16
    )
    d_probs = jnp.dot(d_att, payload_entries.T, preferred_element_type=jnp.float32)
    d_scores = probs * (d_probs - jnp.sum(probs * d_probs, axis=-1, keepdims=True))
    d_scores_b = d_scores.astype(jnp.bfloat16)
    d_query = (scale * jnp.dot(d_scores_b, keys, preferred_element_type=jnp.float32)).astype(
        jnp.bfloat16
    )
    key_part = jnp.einsum("st,sd->td", d_scores_b, query, preferred_element_type=jnp.float32)
    value_part = jnp.einsum("st,sd->td", probs_b, d_att, preferred_element_type=jnp.float32)
    return (mixed_homologs, d_query, key_part, value_part)


def body(
    family_activity,
    rescale_factor,
    asking_weights,
    lookup_weights,
    payload_weights,
    exit_weights,
    upstream_adjoint,
):
    query_weight, key_weight, value_weight, output_matrix = (
        lax.all_gather(asking_weights, ("depth", "res"), axis=0, tiled=True),
        lax.all_gather(lookup_weights, ("depth", "res"), axis=0, tiled=True),
        lax.all_gather(payload_weights, ("depth", "res"), axis=0, tiled=True),
        lax.all_gather(exit_weights, ("depth", "res"), axis=0, tiled=True),
    )
    homologs_each_shard, positions_each_shard, embed_span = family_activity.shape
    standardized_source, standardized_entries, reciprocal_spread = standardize_entries(
        family_activity, rescale_factor
    )
    query = project(standardized_source, query_weight, HEAD_DIM ** (-0.5))
    keys = project(standardized_source, key_weight, 1.0)
    payload_entries = project(standardized_source, value_weight, 1.0)
    keys_all, values_all = (
        lax.all_gather(keys, "depth", axis=0, tiled=True),
        lax.all_gather(payload_entries, "depth", axis=0, tiled=True),
    )
    d_att = jnp.dot(upstream_adjoint, output_matrix.T, preferred_element_type=jnp.float32).astype(
        jnp.bfloat16
    )

    def per_head(items):
        return head_pass(items[0], items[1], items[2], items[3])

    mixed_homologs, d_query, key_part, value_part = lax.map(
        per_head, (to_heads(query), to_heads(keys_all), to_heads(values_all), to_heads(d_att))
    )
    mixed_homologs = from_heads(mixed_homologs, positions_each_shard)
    d_query = from_heads(d_query, positions_each_shard)
    key_part = from_heads(key_part, positions_each_shard)
    value_part = from_heads(value_part, positions_each_shard)
    rows = homologs_each_shard * positions_each_shard
    normed_rows = standardized_source.reshape(rows, embed_span)
    part_query = jnp.dot(
        normed_rows.T, d_query.reshape(rows, embed_span), preferred_element_type=jnp.float32
    )
    part_out = jnp.dot(
        mixed_homologs.reshape(rows, embed_span).T,
        upstream_adjoint.reshape(rows, embed_span),
        preferred_element_type=jnp.float32,
    )
    stacked = jnp.stack([key_part, value_part], axis=2).astype(jnp.bfloat16)
    summed = (
        lax.psum_scatter(stacked, "depth", scatter_dimension=0, tiled=True)
        .astype(jnp.float32)
        .astype(jnp.bfloat16)
    )
    d_keys = summed[:, :, 0, :]
    d_values = summed[:, :, 1, :]
    final_result = (
        family_activity.astype(jnp.float32)
        + jnp.dot(mixed_homologs, output_matrix, preferred_element_type=jnp.float32)
    ).astype(jnp.bfloat16)
    part_key = jnp.dot(
        normed_rows.T, d_keys.reshape(rows, embed_span), preferred_element_type=jnp.float32
    )
    part_value = jnp.dot(
        normed_rows.T, d_values.reshape(rows, embed_span), preferred_element_type=jnp.float32
    )
    d_normed = jnp.dot(d_query, query_weight.T, preferred_element_type=jnp.float32)
    d_normed = d_normed + jnp.dot(d_keys, key_weight.T, preferred_element_type=jnp.float32)
    d_normed = d_normed + jnp.dot(d_values, value_weight.T, preferred_element_type=jnp.float32)
    part_gain = jnp.sum((d_normed * standardized_entries).reshape(rows, embed_span), axis=0)
    unit_gradient = d_normed * rescale_factor
    alignment_gradient = upstream_adjoint.astype(jnp.float32) + reciprocal_spread * (
        unit_gradient
        - jnp.mean(unit_gradient, axis=-1, keepdims=True)
        - standardized_entries
        * jnp.mean(unit_gradient * standardized_entries, axis=-1, keepdims=True)
    )
    query_gradient, key_gradient, value_gradient, output_gradient, gain_gradient = (
        lax.psum_scatter(part_query, ("depth", "res"), scatter_dimension=0, tiled=True),
        lax.psum_scatter(part_key, ("depth", "res"), scatter_dimension=0, tiled=True),
        lax.psum_scatter(part_value, ("depth", "res"), scatter_dimension=0, tiled=True),
        lax.psum_scatter(part_out, ("depth", "res"), scatter_dimension=0, tiled=True),
        lax.psum_scatter(part_gain, ("depth", "res"), scatter_dimension=0, tiled=True),
    )
    return (
        final_result,
        alignment_gradient.astype(jnp.bfloat16),
        query_gradient,
        key_gradient,
        value_gradient,
        output_gradient,
        gain_gradient,
    )


def solution(mesh):
    return jax.shard_map(
        body,
        mesh=mesh,
        in_specs=(
            P("depth", "res", None),
            P(),
            P(("depth", "res"), None),
            P(("depth", "res"), None),
            P(("depth", "res"), None),
            P(("depth", "res"), None),
            P("depth", "res", None),
        ),
        out_specs=(
            P("depth", "res", None),
            P("depth", "res", None),
            P(("depth", "res"), None),
            P(("depth", "res"), None),
            P(("depth", "res"), None),
            P(("depth", "res"), None),
            P(("depth", "res")),
        ),
        check_vma=False,
    )
```

profile of v0, /device:TPU:0, one launch (start us, length us, event | category | flops | bytes accessed | tf_op | source)
XLA Modules:
  0.0 857.8 jit_solution(14415364014940484607)
XLA Ops:
  12.5 55.5 %all-gather.11.cloned.1.call-done = bf16[768,768]{1,0:T(8,128)(2,1)} async-done(((bf16[24,768]{1,0:T(8,128)(2,1)}), bf16[768,768]{1,0:T(8,128)(2,1)}) %all-gather.11.cloned.1.call-update) | async-done | bytes 1179664 | tf_op jit(solution)/shard_map/all_gather | solution.py:70
  67.9 2.7 convolution_convert_fusion.3
  70.7 53.4 %all-gather.13.cloned.1.call-done = bf16[768,768]{1,0:T(8,128)(2,1)} async-done(((bf16[24,768]{1,0:T(8,128)(2,1)}), bf16[768,768]{1,0:T(8,128)(2,1)}) %all-gather.13.cloned.1.call-update) | async-done | bytes 1179664 | tf_op jit(solution)/shard_map/all_gather | solution.py:71
  124.1 2.5 convolution_convert_fusion.2
  126.8 53.5 %all-gather.9.cloned.1.call-done = bf16[768,768]{1,0:T(8,128)(2,1)} async-done(((bf16[24,768]{1,0:T(8,128)(2,1)}), bf16[768,768]{1,0:T(8,128)(2,1)}) %all-gather.9.cloned.1.call-update) | async-done | bytes 1179664 | tf_op jit(solution)/shard_map/all_gather | solution.py:69
  182.3 54.1 %all-gather.15.cloned.1.call-done = bf16[768,768]{1,0:T(8,128)(2,1)} async-done(((bf16[24,768]{1,0:T(8,128)(2,1)}), bf16[768,768]{1,0:T(8,128)(2,1)}) %all-gather.15.cloned.1.call-update) | async-done | bytes 1179664 | tf_op jit(solution)/shard_map/all_gather | solution.py:72
  239.0 29.5 %all-gather.17.cloned.1.call-done = bf16[1024,768]{1,0:T(8,128)(2,1)} async-done(((bf16[256,768]{1,0:T(8,128)(2,1)}), bf16[1024,768]{1,0:T(8,128)(2,1)}) %all-gather.17.cloned.1.call-update) | async-done | bytes 1572880 | tf_op jit(solution)/shard_map/all_gather | solution.py:82
  270.2 31.6 %all-gather.19.cloned.1.call-done = bf16[1024,768]{1,0:T(8,128)(2,1)} async-done(((bf16[256,768]{1,0:T(8,128)(2,1)}), bf16[1024,768]{1,0:T(8,128)(2,1)}) %all-gather.19.cloned.1.call-update) | async-done | bytes 1572880 | tf_op jit(solution)/shard_map/all_gather | solution.py:83
  301.8 2.7 copy.28
  304.5 80.6 %while.16 = (s32[]{:T(128)}, bf16[12,256,64]{1,2,0:T(8,128)(2,1)S(1)}, bf16[12,256,64]{1,2,0:T(8,128)(2,1)S(1)}, bf16[12,1024,64]{1,2,0:T(8,128)(2,1)}, bf16[12,...) while((s32[]{:T(128)}, ...), condition=%wide.region_6.7_spmd, body=%wide.region_2.6_spmd.sunk | while | flops 206093568 | bytes 11226213 | solution.py:92
  305.2 1.8 fusion.110
  311.9 1.8 fusion.110
  318.6 1.8 fusion.110
  325.3 1.8 fusion.110
  332.1 1.8 fusion.110
  345.5 1.8 fusion.110
  352.2 1.8 fusion.110
  358.9 1.8 fusion.110
  365.7 1.8 fusion.110
  372.4 1.8 fusion.110
  385.1 3.8 pad_maximum_fusion
  389.0 2.1 fusion.62
  391.1 1.9 fusion.55
  393.1 39.9 %reduce-scatter.6.cloned.1.call-done = bf16[256,1,2,768]{0,3,2,1:T(8,128)(2,1)} async-done(((bf16[1024,1,2,768]{0,3,2,1:T(8,128)(2,1)}), bf16[256,1,2,768]{0,3,2,1:T(8,128)(2,1)}) %reduce-scatter.6.cloned.1.call-update) | async-done | bytes 786448 | tf_op jit(solution)/shard_map/reduce_scatter | solution.py:111
  433.1 3.0 fusion.58
  437.2 2.1 fusion.59
  441.2 2.6 fusion.38
  445.8 39.4 %all-reduce = f32[768]{0:T(1024)S(1)} all-reduce(f32[768]{0:T(1024)S(1)} %get-tuple-element.79), channel_id=9, replica_groups=mesh['depth'=4,'res'=8] {'depth','res'}, use_global_device_ids=true, to_apply=%region_15.16.clone | all-reduce | flops 768 | bytes 6144
  487.0 50.9 %reduce-scatter.8.cloned.1.call-done = f32[24,768]{1,0:T(8,128)} async-done(((f32[768,768]{1,0:T(8,128)}), f32[24,768]{1,0:T(8,128)}) %reduce-scatter.8.cloned.1.call-update) | async-done | bytes 73744 | tf_op jit(solution)/shard_map/reduce_scatter | solution.py:139
  537.9 104.7 %reduce-scatter.14.cloned.1.call-done = f32[24,768]{1,0:T(8,128)} async-done(((f32[768,768]{1,0:T(8,128)}), f32[24,768]{1,0:T(8,128)}) %reduce-scatter.14.cloned.1.call-update) | async-done | bytes 73744 | tf_op jit(solution)/shard_map/reduce_scatter | solution.py:142
  642.6 103.8 %reduce-scatter.10.cloned.1.call-done = f32[24,768]{1,0:T(8,128)} async-done(((f32[768,768]{1,0:T(8,128)}), f32[24,768]{1,0:T(8,128)}) %reduce-scatter.10.cloned.1.call-update) | async-done | bytes 73744 | tf_op jit(solution)/shard_map/reduce_scatter | solution.py:140
  746.4 104.8 %reduce-scatter.12.cloned.1.call-done = f32[24,768]{1,0:T(8,128)} async-done(((f32[768,768]{1,0:T(8,128)}), f32[24,768]{1,0:T(8,128)}) %reduce-scatter.12.cloned.1.call-update) | async-done | bytes 73744 | tf_op jit(solution)/shard_map/reduce_scatter | solution.py:141
  (140 shorter events, 80.7 us)
Async XLA Ops:
  7.2 60.8 %all-gather.11.cloned.1.call-start = ((), (), s32[]{:S(2)}) async-start(), calls=%async_computation.6 | async-start | bytes 1216512 | tf_op jit(solution)/shard_map/all_gather | solution.py:70
  7.9 116.2 %all-gather.13.cloned.1.call-start = ((), (), s32[]{:S(2)}) async-start(), calls=%async_computation.7 | async-start | bytes 1216512 | tf_op jit(solution)/shard_map/all_gather | solution.py:71
  8.6 171.6 %all-gather.9.cloned.1.call-start = ((), (), s32[]{:S(2)}) async-start(), calls=%async_computation.5 | async-start | bytes 1216512 | tf_op jit(solution)/shard_map/all_gather | solution.py:69
  9.4 226.9 %all-gather.15.cloned.1.call-start = ((), (), s32[]{:S(2)}) async-start(), calls=%async_computation.8 | async-start | bytes 1216512 | tf_op jit(solution)/shard_map/all_gather | solution.py:72
  10.0 258.6 %all-gather.17.cloned.1.call-start = ((), (), s32[]{:S(2)}) async-start(), calls=%async_computation.14 | async-start | bytes 1966080 | tf_op jit(solution)/shard_map/all_gather | solution.py:82
  11.1 113.0 %copy-start = (bf16[256,1,768]{2,0,1:T(8,128)(2,1)S(1)}, bf16[256,1,768]{2,0,1:T(8,128)(2,1)}, u32[]{:S(2)}) copy-start(bf16[256,1,768]{2,0,1:T(8,128)(2,1)} %param.9) | copy-start | bytes 1179652
  11.2 113.0 %copy-start.4 = (f32[768]{0:T(1024)S(1)}, f32[768]{0:T(1024)}, u32[]{:S(2)}) copy-start(f32[768]{0:T(1024)} %param.10) | copy-start | bytes 9220
  70.6 231.2 %all-gather.19.cloned.1.call-start = ((), (), s32[]{:S(2)}) async-start(), calls=%async_computation.15 | async-start | bytes 1966080 | tf_op jit(solution)/shard_map/all_gather | solution.py:83
  126.7 306.4 %reduce-scatter.6.cloned.1.call-start = ((), (), s32[]{:S(2)}) async-start(), calls=%async_computation.9 | async-start | bytes 3932160 | tf_op jit(solution)/shard_map/reduce_scatter | solution.py:111
  126.8 109.6 %copy-start.1 = (bf16[256,1,768]{2,0,1:T(8,128)(2,1)S(1)}, bf16[256,1,768]{2,0,1:T(8,128)(2,1)}, u32[]{:S(2)}) copy-start(bf16[256,1,768]{2,0,1:T(8,128)(2,1)} %param.15) | copy-start | bytes 1179652
  388.9 149.0 %reduce-scatter.8.cloned.1.call-start = ((), (), s32[]{:S(2)}) async-start(), calls=%async_computation.10 | async-start | bytes 2433024 | tf_op jit(solution)/shard_map/reduce_scatter | solution.py:139
  391.1 251.5 %reduce-scatter.14.cloned.1.call-start = ((), (), s32[]{:S(2)}) async-start(), calls=%async_computation.13 | async-start | bytes 2433024 | tf_op jit(solution)/shard_map/reduce_scatter | solution.py:142
  393.1 353.4 %reduce-scatter.10.cloned.1.call-start = ((), (), s32[]{:S(2)}) async-start(), calls=%async_computation.11 | async-start | bytes 2433024 | tf_op jit(solution)/shard_map/reduce_scatter | solution.py:140
  436.1 1.1 copy-start.2
  436.1 415.1 %reduce-scatter.12.cloned.1.call-start = ((), (), s32[]{:S(2)}) async-start(), calls=%async_computation.12 | async-start | bytes 2433024 | tf_op jit(solution)/shard_map/reduce_scatter | solution.py:141
  441.2 2.6 copy-start.3
  443.8 1.3 copy-start.5
Sparse Core Ops, SparseCore 0:
  11.0 56.8 all-gather.10
  70.9 53.1 all-gather.12
  127.1 53.1 all-gather.8
  183.2 53.1 all-gather.14
  238.6 29.9 all-gather.16
  270.8 30.9 all-gather.18
  389.1 43.9 reduce-scatter.5
  438.9 98.9 reduce-scatter.7
  544.7 97.9 reduce-scatter.13
  648.3 98.0 reduce-scatter.9
  753.2 98.0 reduce-scatter.11
where the time goes:
time: 860 us; the launch traced here: 858 us
  waiting for transfers between devices  684 us (80%)
  matrix products  96.2 us (11%)
  blocking collectives  39.4 us (5%)
  other arithmetic  15.1 us (2%)
  between operations  14 us (2%)
    reduce_scatter x1, waiting for transfers between devices, body(): lax.psum_scatter(part_value, ('depth', 'res'), scatter_dimension=0, tiled...  105 us
    reduce_scatter x1, waiting for transfers between devices, body(): lax.psum_scatter(part_out, ('depth', 'res'), scatter_dimension=0, tiled=T...  105 us
    reduce_scatter x1, waiting for transfers between devices, body(): lax.psum_scatter(part_key, ('depth', 'res'), scatter_dimension=0, tiled=T...  104 us
    all_gather x1, waiting for transfers between devices, body(): lax.all_gather(lookup_weights, ('depth', 'res'), axis=0, tiled=True)  55.5 us
    all_gather x1, waiting for transfers between devices, body(): lax.all_gather(exit_weights, ('depth', 'res'), axis=0, tiled=True)  54.1 us
    all_gather x1, waiting for transfers between devices, body(): lax.all_gather(asking_weights, ('depth', 'res'), axis=0, tiled=True)  53.5 us
    all_gather x1, waiting for transfers between devices, body(): lax.all_gather(payload_weights, ('depth', 'res'), axis=0, tiled=True)  53.4 us
    reduce_scatter x1, waiting for transfers between devices, body(): lax.psum_scatter(part_query, ('depth', 'res'), scatter_dimension=0, tiled...  50.9 us
  transfers between devices with their start and end apart: 11, of which 11 were waited for; matrix products, arithmetic and copies ran while one was open for 4% of the time, Pallas kernels for 0%

commit v1 on v0

--- a/solution.py
+++ b/solution.py
@@ -1,7 +1,11 @@
+import functools
+
 import jax
 import jax.numpy as jnp
 from jax import lax
-from jax.sharding import PartitionSpec as P
+from jax.experimental import pallas as pl
+from jax.experimental.pallas import tpu as pltpu
+from jax.sharding import Mesh, PartitionSpec as P
 
 HEADS = 12
 HEAD_DIM = 64
@@ -56,7 +60,7 @@
     return (mixed_homologs, d_query, key_part, value_part)
 
 
-def body(
+def general_body(
     family_activity,
     rescale_factor,
     asking_weights,
@@ -64,12 +68,13 @@
     payload_weights,
     exit_weights,
     upstream_adjoint,
+    axes=("depth", "res"),
 ):
     query_weight, key_weight, value_weight, output_matrix = (
-        lax.all_gather(asking_weights, ("depth", "res"), axis=0, tiled=True),
-        lax.all_gather(lookup_weights, ("depth", "res"), axis=0, tiled=True),
-        lax.all_gather(payload_weights, ("depth", "res"), axis=0, tiled=True),
-        lax.all_gather(exit_weights, ("depth", "res"), axis=0, tiled=True),
+        lax.all_gather(asking_weights, axes, axis=0, tiled=True),
+        lax.all_gather(lookup_weights, axes, axis=0, tiled=True),
+        lax.all_gather(payload_weights, axes, axis=0, tiled=True),
+        lax.all_gather(exit_weights, axes, axis=0, tiled=True),
     )
     homologs_each_shard, positions_each_shard, embed_span = family_activity.shape
     standardized_source, standardized_entries, reciprocal_spread = standardize_entries(
@@ -136,11 +141,11 @@
         * jnp.mean(unit_gradient * standardized_entries, axis=-1, keepdims=True)
     )
     query_gradient, key_gradient, value_gradient, output_gradient, gain_gradient = (
-        lax.psum_scatter(part_query, ("depth", "res"), scatter_dimension=0, tiled=True),
-        lax.psum_scatter(part_key, ("depth", "res"), scatter_dimension=0, tiled=True),
-        lax.psum_scatter(part_value, ("depth", "res"), scatter_dimension=0, tiled=True),
-        lax.psum_scatter(part_out, ("depth", "res"), scatter_dimension=0, tiled=True),
-        lax.psum_scatter(part_gain, ("depth", "res"), scatter_dimension=0, tiled=True),
+        lax.psum_scatter(part_query, axes, scatter_dimension=0, tiled=True),
+        lax.psum_scatter(part_key, axes, scatter_dimension=0, tiled=True),
+        lax.psum_scatter(part_value, axes, scatter_dimension=0, tiled=True),
+        lax.psum_scatter(part_out, axes, scatter_dimension=0, tiled=True),
+        lax.psum_scatter(part_gain, axes, scatter_dimension=0, tiled=True),
     )
     return (
         final_result,
@@ -153,27 +158,352 @@
     )
 
 
+F32, BF16 = jnp.float32, jnp.bfloat16
+SCALE = HEAD_DIM ** (-0.5)
+
+
+def swap(value, axis, size, bits):
+    return lax.ppermute(value, axis, [(i, i ^ bits) for i in range(size)])
+
+
+def dot(a, b, contract=(1, 0)):
+    return lax.dot_general(
+        a, b, (((contract[0],), (contract[1],)), ((), ())), preferred_element_type=F32
+    )
+
+
+def unit_rows(x):
+    x = x.astype(F32)
+    centered = x - jnp.mean(x, axis=-1, keepdims=True)
+    inverse = lax.rsqrt(jnp.mean(centered * centered, axis=-1, keepdims=True) + 1e-05)
+    return centered * inverse, inverse
+
+
+def head_masks(span):
+    lane = lax.broadcasted_iota(jnp.int32, (8, span), 1)
+    return [
+        ((lane >= at) & (lane < at + HEAD_DIM)).astype(F32)[0:1].astype(BF16)
+        for at in range(0, span, HEAD_DIM)
+    ]
+
+
+def pack_kernel(dims, w_query, w_key, w_value, out):
+    depth, zs, shard, block, span = dims
+    for d in range(depth):
+        lanes = slice(d * span, (d + 1) * span)
+        for i, w in enumerate((w_query, w_key, w_value)):
+            part = w[:, lanes]
+            for z in range(zs):
+                out[d * zs + z, :, i * span : (i + 1) * span] = part
+
+
+def forward_kernel(dims, *refs):
+    depth, zs, shard, block, span = dims
+    heads = span // HEAD_DIM
+    core, refs = refs[0], refs[1:]
+    xs, refs = refs[:depth], refs[depth:]
+    gain, w_near, w_far, w_out, normed, query, keys, values, keys_t, att_t, lse, weights = refs[:12]
+    outs, values_t = refs[12 : 12 + depth], refs[12 + depth]
+
+    first = core[0] == 0
+    for i in range(depth * zs):
+        near, far = w_near[i].astype(F32), w_far[i].astype(F32)
+        weights[i * 2 * shard : (i + 1) * 2 * shard, :] = jnp.concatenate(
+            [jnp.where(first, near, far), jnp.where(first, far, near)], axis=0
+        ).astype(BF16)
+
+    for j in range(depth):
+        rows = slice(j * block, (j + 1) * block)
+        unit, _ = unit_rows(xs[j][...])
+        low = (unit * gain[...]).astype(BF16)
+        normed[rows, :] = low
+        qkv = dot(low, weights[...])
+        query[rows, :] = (SCALE * qkv[:, :span]).astype(BF16)
+        key, value = qkv[:, span : 2 * span], qkv[:, 2 * span :]
+        keys[rows, :] = key.astype(BF16)
+        values[rows, :] = value.astype(BF16)
+        keys_t[:, rows] = jnp.transpose(key).astype(BF16)
+        values_t[:, rows] = jnp.transpose(value).astype(BF16)
+
+    masks = head_masks(span)
+
+    def step(j, _):
+        cols = pl.ds(pl.multiple_of(j * block, block), block)
+        q_block = query[cols, :]
+
+        def score(h):
+            return dot(keys[...], q_block * masks[h], (1, 1))
+
+        scores = [score(h) for h in range(min(2, heads))]
+        for h in range(heads):
+            top = jnp.max(scores[h], axis=0, keepdims=True)
+            e = jnp.exp(scores[h] - top)
+            total = jnp.sum(e, axis=0, keepdims=True)
+            probs = (e * (1.0 / total)).astype(BF16)
+            if h + 2 < heads:
+                scores.append(score(h + 2))
+            lanes = slice(h * HEAD_DIM, (h + 1) * HEAD_DIM)
+            att_t[lanes, cols] = dot(values_t[lanes, :], probs).astype(BF16)
+            lse[h, :, cols] = top + jnp.log(total)
+        return 0
+
+    lax.fori_loop(0, depth, step, 0)
+    for j in range(depth):
+        att = jnp.transpose(att_t[:, j * block : (j + 1) * block].astype(F32)).astype(BF16)
+        outs[j][...] = dot(att, w_out[...]).astype(BF16)
+
+
+def out_grad_kernel(dims, *refs):
+    depth, zs, shard, block, span = dims
+    gs, (att_t, out) = refs[:depth], refs[depth:]
+    total = dot(att_t[:, :block], gs[0][...])
+    for j in range(1, depth):
+        total = total + dot(att_t[:, j * block : (j + 1) * block], gs[j][...])
+    out[...] = total
+
+
+def backward_kernel(dims, *refs):
+    depth, zs, shard, block, span = dims
+    heads = span // HEAD_DIM
+    gs, refs = refs[:depth], refs[depth:]
+    w_out, query, keys, values, keys_t, lse, d_qkv, d_att, d_query_t, d_keys, d_values = refs
+
+    for j in range(depth):
+        rows = slice(j * block, (j + 1) * block)
+        d_att[rows, :] = dot(gs[j][...], w_out[...], (1, 1)).astype(BF16)
+    d_keys[...] = jnp.zeros_like(d_keys)
+    d_values[...] = jnp.zeros_like(d_values)
+    masks = head_masks(span)
+
+    def step(j, _):
+        cols = pl.ds(pl.multiple_of(j * block, block), block)
+        q_block, g_block = query[cols, :], d_att[cols, :]
+        qs = [q_block * m for m in masks]
+        ds = [g_block * m for m in masks]
+
+        def pair(h):
+            return dot(keys[...], qs[h], (1, 1)), dot(values[...], ds[h], (1, 1))
+
+        pairs = [pair(h) for h in range(min(2, heads))]
+        key_part = value_part = None
+        for h in range(heads):
+            scores, d_probs = pairs[h]
+            probs = jnp.exp(scores - lse[h, :, cols])
+            mean = jnp.sum(probs * d_probs, axis=0, keepdims=True)
+            d_scores = (probs * (d_probs - mean)).astype(BF16)
+            if h + 2 < heads:
+                pairs.append(pair(h + 2))
+            values_add = dot(probs.astype(BF16), ds[h])
+            keys_add = dot(d_scores, qs[h])
+            value_part = values_add if h == 0 else value_part + values_add
+            key_part = keys_add if h == 0 else key_part + keys_add
+            lanes = slice(h * HEAD_DIM, (h + 1) * HEAD_DIM)
+            d_query_t[lanes, cols] = SCALE * dot(keys_t[lanes, :], d_scores)
+        d_values[...] += value_part.astype(BF16).astype(F32)
+        d_keys[...] += key_part.astype(BF16).astype(F32)
+        return 0
+
+    lax.fori_loop(0, depth, step, 0)
+    d_qkv[:, span : 2 * span] = d_keys[...].astype(BF16)
+    d_qkv[:, 2 * span :] = d_values[...].astype(BF16)
+    for j in range(depth):
+        rows = slice(j * block, (j + 1) * block)
+        d_qkv[rows, :span] = jnp.transpose(d_query_t[:, rows]).astype(BF16)
+
+
+def weight_kernel(dims, core, gain, normed, d_qkv, weights, near, far):
+    depth, zs, shard, block, span = dims
+    grads = dot(normed[...], d_qkv[...], (0, 0))
+    gain_rows = jnp.transpose(jnp.broadcast_to(gain[...], (128, gain.shape[1])))[:, :64]
+    both = jnp.sum(weights[...].astype(F32) * grads, axis=1, keepdims=True)
+    gain_column = both / gain_rows
+    first = core[0] == 0
+    for i in range(depth * zs):
+        one = slice(2 * i * shard, (2 * i + 1) * shard)
+        two = slice((2 * i + 1) * shard, (2 * i + 2) * shard)
+        near[i, :, : 3 * span] = jnp.where(first, grads[one], grads[two])
+        near[i, :, 3 * span :] = jnp.where(first, gain_column[one], gain_column[two])
+        far[i, :, : 3 * span] = jnp.where(first, grads[two], grads[one]).astype(BF16)
+        far[i, :, 3 * span :] = jnp.where(first, gain_column[two], gain_column[one]).astype(BF16)
+
+
+def input_kernel(dims, weights, d_qkv, *dns):
+    depth, zs, shard, block, span = dims
+    for j in range(depth):
+        rows = slice(j * block, (j + 1) * block)
+        dns[j][...] = dot(d_qkv[rows, :], weights[...], (1, 1)).astype(BF16)
+
+
+def finish_kernel(dims, parts, *outs):
+    depth, zs, shard, block, span = dims
+    gain_sum = None
+    for d in range(depth):
+        total = parts[d * zs].astype(F32)
+        for z in range(1, zs):
+            total = total + parts[d * zs + z].astype(F32)
+        for i in range(3):
+            outs[i][:, d * span : (d + 1) * span] = total[:, i * span : (i + 1) * span]
+        gain = total[:, 3 * span : 3 * span + 1]
+        gain_sum = gain if gain_sum is None else gain_sum + gain
+    wide = jnp.concatenate([gain_sum, jnp.zeros((128 - shard, 1), F32)], axis=0)
+    outs[3][...] = jnp.transpose(jnp.broadcast_to(wide, (128, 128)))[0:8, :]
+
+
+def call(kernel, dims, outs, scratch, args, flops, mib, scalars=0):
+    smem = pl.BlockSpec(memory_space=pltpu.SMEM)
+    vmem = pl.BlockSpec(memory_space=pltpu.VMEM)
+    outs = [jax.ShapeDtypeStruct(shape, kind) for shape, kind in outs]
+    size = sum(a.size * a.dtype.itemsize for a in list(args) + outs)
+    return pl.pallas_call(
+        functools.partial(kernel, dims),
+        out_shape=outs,
+        in_specs=[smem] * scalars + [vmem] * (len(args) - scalars),
+        out_specs=[vmem] * len(outs),
+        scratch_shapes=[pltpu.VMEM(shape, kind) for shape, kind in scratch],
+        compiler_params=pltpu.CompilerParams(vmem_limit_bytes=mib * 1024 * 1024),
+        cost_estimate=pl.CostEstimate(flops=flops, bytes_accessed=size, transcendentals=0),
+    )(*args)
+
+
+def head_body(depth, res, *args):
+    x, gain, w_query, w_key, w_value, w_out, upstream = args
+    homologs, _, width = x.shape
+    span, zs = width // depth, res // 2
+    shard = w_query.shape[0]
+    total, heads = homologs * depth, span // HEAD_DIM
+    dims = (depth, zs, shard, homologs, span)
+    x = x.reshape(homologs, width)
+    upstream = upstream.reshape(homologs, width)
+    gain = gain.reshape(1, width)
+    core = lax.axis_index("core").astype(jnp.int32).reshape(1)
+
+    xs = [x] + [swap(x, "depth", depth, k) for k in range(1, depth)]
+    gs = [upstream] + [swap(upstream, "depth", depth, k) for k in range(1, depth)]
+
+    blocks = depth * zs
+    packed = call(
+        pack_kernel,
+        dims,
+        [((blocks, shard, 3 * span), BF16)],
+        [],
+        [w_query, w_key, w_value],
+        1000,
+        16,
+    )[0]
+    w_near = lax.all_to_all(packed, ("depth", "z"), 0, 0, tiled=True)
+    w_far = swap(w_near, "core", 2, 1)
+    w_out = lax.all_gather(w_out, ("z", "core"), axis=0, tiled=True)
+
+    rows = ((total, span), BF16)
+    turned = ((span, total), BF16)
+    block = ((homologs, width), BF16)
+    pass_flops = 2 * total * total * span
+    normed, query, keys, values, keys_t, att_t, lse, weights, *outs = call(
+        forward_kernel,
+        dims,
+        [((total, width), BF16), rows, rows, rows, turned, turned]
+        + [((heads, 1, total), F32), ((width, 3 * span), BF16)]
+        + [block] * depth,
+        [turned],
+        [core] + xs + [gain, w_near, w_far, w_out],
+        8 * pass_flops,
+        28,
+        scalars=1,
+    )
+
+    grad_out = call(
+        out_grad_kernel, dims, [((span, width), F32)], [], gs + [att_t], 2 * total * width * span, 16
+    )[0]
+    lse, grad_out = lax.optimization_barrier((lse, grad_out))
+    grad_out = lax.psum_scatter(grad_out, ("z", "core"), scatter_dimension=0, tiled=True)
+
+    d_qkv = call(
+        backward_kernel,
+        dims,
+        [((total, 3 * span), BF16)],
+        [rows, ((span, total), F32)] + [((total, span), F32)] * 2,
+        gs + [w_out, query, keys, values, keys_t, lse],
+        24 * pass_flops,
+        28,
+    )[0]
+
+    outs = [outs[0]] + [swap(outs[k], "depth", depth, k) for k in range(1, depth)]
+    d_qkv, *outs = lax.optimization_barrier([d_qkv] + outs)
+    final_result = (x.astype(F32) + sum(o.astype(F32) for o in outs)).astype(BF16)
+
+    lanes = 3 * span + 64
+    near, far = call(
+        weight_kernel,
+        dims,
+        [((blocks, shard, lanes), F32), ((blocks, shard, lanes), BF16)],
+        [],
+        [core, gain, normed, d_qkv, weights],
+        6 * total * width * span,
+        28,
+        scalars=1,
+    )
+    far, d_qkv = lax.optimization_barrier((far, d_qkv))
+    far = swap(far, "core", 2, 1)
+    dns = call(
+        input_kernel, dims, [block] * depth, [], [weights, d_qkv], 6 * total * width * span, 16
+    )
+    near = (near + far.astype(F32)).astype(BF16)
+    near, *dns = lax.optimization_barrier([near] + list(dns))
+    parts = lax.all_to_all(near, ("depth", "z"), 0, 0, tiled=True)
+    dns = [dns[0]] + [swap(dns[k], "depth", depth, k) for k in range(1, depth)]
+    parts, *dns = lax.optimization_barrier([parts] + dns)
+
+    grad_query, grad_key, grad_value, gain_rows = call(
+        finish_kernel,
+        dims,
+        [((shard, width), F32)] * 3 + [((8, 128), F32)],
+        [],
+        [parts],
+        1000,
+        16,
+    )
+
+    d_normed = sum(d.astype(F32) for d in dns)
+    unit, inverse = unit_rows(x)
+    d_unit = d_normed * gain
+    alignment = upstream.astype(F32) + inverse * (
+        d_unit
+        - jnp.mean(d_unit, axis=-1, keepdims=True)
+        - unit * jnp.mean(d_unit * unit, axis=-1, keepdims=True)
+    )
+    return (
+        final_result.reshape(homologs, 1, width),
+        alignment.astype(BF16).reshape(homologs, 1, width),
+        grad_query,
+        grad_key,
+        grad_value,
+        grad_out,
+        gain_rows[0, :shard],
+    )
+
+
 def solution(mesh):
+    depth, res = mesh.shape["depth"], mesh.shape["res"]
+    powers = depth & (depth - 1) == 0 and res & (res - 1) == 0 and res > 1
+    if powers and HEADS % depth == 0:
+        axes = ("depth", "z", "core")
+        mesh = Mesh(mesh.devices.reshape(depth, res // 2, 2), axes)
+        res_axes, run = ("z", "core"), functools.partial(head_body, depth, res)
+    else:
+        axes = ("depth", "res")
+        res_axes, run = ("res",), general_body
+
+    def body(*args):
+        if args[0].shape[1] != 1:
+            return general_body(*args, axes=axes)
+        return run(*args)
+
+    rows = P("depth", res_axes, None)
+    weight = P(axes, None)
     return jax.shard_map(
         body,
         mesh=mesh,
-        in_specs=(
-            P("depth", "res", None),
-            P(),
-            P(("depth", "res"), None),
-            P(("depth", "res"), None),
-            P(("depth", "res"), None),
-            P(("depth", "res"), None),
-            P("depth", "res", None),
-        ),
-        out_specs=(
-            P("depth", "res", None),
-            P("depth", "res", None),
-            P(("depth", "res"), None),
-            P(("depth", "res"), None),
-            P(("depth", "res"), None),
-            P(("depth", "res"), None),
-            P(("depth", "res")),
-        ),
+        in_specs=(rows, P(), weight, weight, weight, weight, rows),
+        out_specs=(rows, rows, weight, weight, weight, weight, P(axes)),
         check_vma=False,
     )

time: 860 us -> 153 us (0.18)
  waiting for transfers between devices: 684 us -> 40 us
  matrix products: 96.2 us -> 0 us
  Pallas kernels: 0 us -> 28.3 us
  starting transfers between devices: 0.44 us -> 28.4 us
  blocking collectives: 39.4 us -> 14.2 us
  local copies, waits for them, and re-layouts: 7.89 us -> 21.8 us
  other arithmetic: 15.1 us -> 5.37 us
    reduce_scatter x5 -> x1, waiting for transfers between devices: 404 us -> 5.48 us  [head_body(): lax.psum_scatter(grad_out, ('z', 'core'), scatter_dimension=0, tiled=True)]
    all_gather x6 -> x0, waiting for transfers between devices: 278 us -> none  [the longest x1 55.5 us: body(): lax.all_gather(lookup_weights, ('depth', 'res'), axis=0, tiled=True)]
    dot_general x84 -> x0, matrix products: 96.2 us -> none  [the longest x12 21.8 us: head_pass(): jnp.einsum('st,sd->td', probs_b, d_att, preferred_element_type=jnp.float32)]
    unnamed x1 -> x0, blocking collectives: 39.4 us -> none
    pallas_call x0 -> x7, Pallas kernels: none -> 28.3 us  [call(): pl.pallas_call(functools.partial(kernel, dims), out_shape=outs, in_specs=...]
    ppermute x0 -> x14, waiting for transfers between devices: none -> 22.3 us  [swap(): return lax.ppermute(value, axis, [(i, i ^ bits) for i in range(size)])]
    unnamed x13 -> x68, local copies, waits for them, and re-layouts: 2.42 us -> 21.2 us
    ppermute x0 -> x14, starting transfers between devices: none -> 14.6 us  [swap(): return lax.ppermute(value, axis, [(i, i ^ bits) for i in range(size)])]
  transfers between devices with their start and end apart: 11 -> 17, of which waited for: 11 -> 7; matrix products, arithmetic and copies ran while one was open for 4% -> 3% of each run, Pallas kernels for 0% -> 15%
where the time goes in v1:
time: 153 us; the launch traced here: 152 us
  waiting for transfers between devices  40 us (26%)
  starting transfers between devices  28.4 us (19%)
  Pallas kernels  28.3 us (18%)
  local copies, waits for them, and re-layouts  21.8 us (14%)
  blocking collectives  14.2 us (9%)
  between operations  14.2 us (9%)
  other arithmetic  5.37 us (4%)
    pallas_call x7, Pallas kernels, call(): pl.pallas_call(functools.partial(kernel, dims), out_shape=outs, in_specs=...  28.3 us
    ppermute x14, waiting for transfers between devices, swap(): return lax.ppermute(value, axis, [(i, i ^ bits) for i in range(size)])  22.3 us
    unnamed x68, local copies, waits for them, and re-layouts  21.2 us
    ppermute x14, starting transfers between devices, swap(): return lax.ppermute(value, axis, [(i, i ^ bits) for i in range(size)])  14.6 us
    all_gather x1, blocking collectives, head_body(): w_out = lax.all_gather(w_out, ('z', 'core'), axis=0, tiled=True)  14.2 us
    all_to_all x1, waiting for transfers between devices, head_body(): w_near = lax.all_to_all(packed, ('depth', 'z'), 0, 0, tiled=True)  12.2 us
    all_to_all x1, starting transfers between devices, head_body(): w_near = lax.all_to_all(packed, ('depth', 'z'), 0, 0, tiled=True)  8.31 us
    reduce_scatter x1, waiting for transfers between devices, head_body(): lax.psum_scatter(grad_out, ('z', 'core'), scatter_dimension=0, tiled=True)  5.48 us
  transfers between devices with their start and end apart: 17, of which 7 were waited for; matrix products, arithmetic and copies ran while one was open for 3% of the time, Pallas kernels for 15%

profile of v1, /device:TPU:0, one launch (start us, length us, event | category | flops | bytes accessed | tf_op | source)
XLA Modules:
  0.0 152.2 jit_solution(16224137987234429563)
XLA Ops:
  10.4 8.3 %all-to-all-start = ((bf16[16,24,576]{2,1,0:T(8,128)(2,1)}), bf16[16,24,576]{2,1,0:T(8,128)(2,1)S(1)}, u32[]{:S(2)}, u32[]{:S(2)}) async-start(bf16[16,24,576]{2,1,0:T(8,128)(2,1)} %shard_map.126), calls=%async_computation | async-start | bytes 983040 | tf_op jit(solution)/shard_map/all_to_all | solution.py:393
  18.8 2.0 %collective-permute-start.3 = (bf16[256,768]{1,0:T(8,128)(2,1)S(1)}, bf16[256,768]{1,0:T(8,128)(2,1)S(1)}, u32[]{:S(2)}, u32[]{:S(2)}) collective-permute-start(bf16[256,768]{1,0:T(8,128)(2,1)S(1)} %bitcast.15), channel_id=1, source_target_pairs={{0,8},{8,0},{16,24},{24,16},{1,9},{9,1},{17,25},{25,17},{2,10},{10... | collective-permute-start | bytes 1179656 | tf_op jit(solution)/shard_map/ppermute | solution.py:166
  20.8 1.5 collective-permute-start.4
  22.2 12.2 %all-to-all-done.refs_6_ = bf16[16,24,576]{2,1,0:T(8,128)(2,1)S(1)} async-done(((bf16[16,24,576]{2,1,0:T(8,128)(2,1)}), bf16[16,24,576]{2,1,0:T(8,128)(2,1)S(1)}, u32[]{:S(2)}, u32[]{:S(2)}) %all-to-all-start) | async-done | bytes 442400 | tf_op jit(solution)/shard_map/all_to_all | solution.py:393
  34.9 1.5 collective-permute-start
  37.2 1.5 collective-permute-start.1
  39.9 14.2 %all_gather.3.refs_8_.refs_4_ = bf16[192,768]{1,0:T(8,128)(2,1)S(1)} all-gather(bf16[24,768]{1,0:T(8,128)(2,1)S(1)} %copy-done.31), channel_id=1, replica_groups=mesh['depth'=4,'z'=4,'core'=2] {'z','core'}, dimensions={0}, use_global_device_ids=true | all-gather | bytes 331776 | tf_op jit(solution)/shard_map/all_gather | solution.py:395
  55.7 1.0 copy-done.12
  56.7 1.0 copy-done.14
  57.7 1.0 copy-done.16
  58.7 1.0 copy-done.18
  59.7 9.5 %shard_map.127 = (bf16[1024,768]{1,0:T(8,128)(2,1)S(1)}, bf16[1024,192]{1,0:T(8,128)(2,1)S(1)}, bf16[1024,192]{1,0:T(8,128)(2,1)S(1)}, bf16[1024,192]{1,0:T(8,12...) custom-call(s32[1]{0:T(128)} %bitcast.2.refs_0_.core, ...), custom_call_target="tpu_custom_call" | custom-call | flops 3221225472 | bytes 8764420 | tf_op jit(solution)/shard_map/pallas_call | solution.py:357
  73.4 2.3 %shard_map.128 = f32[192,768]{1,0:T(8,128)} custom-call(bf16[256,768]{1,0:T(8,128)(2,1)S(1)} %bitcast.22, bf16[256,768]{1,0:T(8,128)(2,1)} %collective-permute-done.refs_1_, bf16[256,768]{1,0:T(8,128)(2,1)S(1)} %collective-permute-done.1.refs_2_, bf16[256,768]{1,0:T(8,128)(2,1)S(1)} %collective-permute-done.2.refs_3_, ...), custom_call_target="tpu_custom_call" | custom-call | flops 301989888 | bytes 2555904 | tf_op jit(solution)/shard_map/pallas_call | solution.py:357
  77.2 1.5 collective-permute-start.7
  78.7 1.5 collective-permute-start.8
  80.7 1.0 copy-done.5
  81.7 1.0 copy-done.7
  82.7 1.0 copy-done.20
  83.7 1.0 copy-done.22
  84.8 1.0 copy-done.24
  85.8 1.0 copy-done.26
  86.8 11.3 %shard_map.129.d_qkv = bf16[1024,576]{1,0:T(8,128)(2,1)S(1)} custom-call(bf16[256,768]{1,0:T(8,128)(2,1)S(1)} %bitcast.23, bf16[256,768]{1,0:T(8,128)(2,1)} %collective-permute-done.refs_1_, bf16[256,768]{1,0:T(8,128)(2,1)S(1)} %copy-done.5, bf16[256,768]{1,0:T(8,128)(2,1)S(1)} %copy-done.7, bf16[192,768]{1,0:T(8,128)(2,1)S(1)} %all_gather.3.refs_8_.refs_4_, ...), custom_call_target="tpu_custom_call" | custom-call | flops 9663676416 | bytes 4632576 | tf_op jit(solution)/shard_map/pallas_call | solution.py:357
  98.4 2.0 %shard_map.130 = (f32[16,24,640]{2,1,0:T(8,128)S(1)}, bf16[16,24,640]{2,1,0:T(8,128)(2,1)S(1)}) custom-call(s32[1]{0:T(128)} %bitcast.2.refs_0_.core, f32[1,768]{1,0:T(1,128)S(1)} %reshape.56.refs_5_.gain, bf16[1024,768]{1,0:T(8,128)(2,1)S(1)} %get-tuple-element.63.normed, bf16[1024,576]{1,0:T(8,128)(2,1)S(1)} %shard_map.129.d_qkv, ...), custom_call_target="tpu_custom_call" | custom-call | flops 905969664 | bytes 5114884 | tf_op jit(solution)/shard_map/pallas_call | solution.py:357
  100.6 1.4 shard_map.131
  103.3 5.5 %all-to-all-start.1 = ((bf16[16,24,640]{2,1,0:T(8,128)(2,1)}), bf16[16,24,640]{2,1,0:T(8,128)(2,1)S(1)}, u32[]{:S(2)}, u32[]{:S(2)}) async-start(bf16[16,24,640]{2,1,0:T(8,128)(2,1)} %add_convert_fusion), calls=%async_computation.1 | async-start | bytes 983040 | tf_op jit(solution)/shard_map/all_to_all | solution.py:452
  109.0 2.0 %collective-permute-start.11 = (bf16[256,768]{1,0:T(8,128)(2,1)S(1)}, bf16[256,768]{1,0:T(8,128)(2,1)}, u32[]{:S(2)}, u32[]{:S(2)}) collective-permute-start(bf16[256,768]{1,0:T(8,128)(2,1)S(1)} %get-tuple-element.76), channel_id=1, source_target_pairs={{0,8},{8,0},{16,24},{24,16},{1,9},{9,1},{17,25},{25,17},{2,10},{10... | collective-permute-start | bytes 1179656 | tf_op jit(solution)/shard_map/ppermute | solution.py:166
  111.0 1.5 collective-permute-start.12
  112.8 13.3 %collective-permute-done.11 = bf16[256,768]{1,0:T(8,128)(2,1)} collective-permute-done((bf16[256,768]{1,0:T(8,128)(2,1)S(1)}, bf16[256,768]{1,0:T(8,128)(2,1)}, u32[]{:S(2)}, u32[]{:S(2)}) %collective-permute-start.11) | collective-permute-done | bytes 393248 | tf_op jit(solution)/shard_map/ppermute | solution.py:166
  126.4 8.1 %collective-permute-done.13 = bf16[256,768]{1,0:T(8,128)(2,1)} collective-permute-done((bf16[256,768]{1,0:T(8,128)(2,1)S(1)}, bf16[256,768]{1,0:T(8,128)(2,1)}, u32[]{:S(2)}, u32[]{:S(2)}) %collective-permute-start.13) | collective-permute-done | bytes 393248 | tf_op jit(solution)/shard_map/ppermute | solution.py:166
  135.3 1.7 %fusion.13 = (f32[256]{0:T(256)S(1)}, f32[256]{0:T(256)S(1)}, f32[256,768]{1,0:T(8,128)S(1)}) fusion(f32[256]{0:T(256)S(1)} %add_rsqrt_fusion, f32[256]{0:T(256)S(1)} %broadcast_multiply_fusion.2, bf16[256,1,768]{2,0,1:T(8,128)(2,1)S(1)} %copy-done, f32[768]{0:T(1024)S(1)} %copy-done.33, bf16[256,768]{1,0:T(8,128)(2,1)} %collective-permute-done.13, ...), kind=kLoop, calls=%fused_computation.23 | loop fusion | flops 2752000 | bytes 2759680 | tf_op jit(solution)/shard_map/reduce_sum | solution.py:471
  137.5 2.4 %fusion.12 = (bf16[256,1,768]{2,0,1:T(8,128)(2,1)}, bf16[256,1,768]{2,0,1:T(8,128)(2,1)}) fusion(f32[256,768]{1,0:T(8,128)S(1)} %get-tuple-element.91, f32[256]{0:T(256)S(1)} %get-tuple-element.94, f32[256]{0:T(256)S(1)} %get-tuple-element.95, f32[256]{0:T(256)S(1)} %add_rsqrt_fusion, f32[256]{0:T(256)S(1)} %broadcast_multiply_fusion.2, ...), kind=kLoop, calls=%fused_computation.17 | loop fusion | flops 3735552 | bytes 3936256 | tf_op jit(solution)/shard_map/reshape | solution.py:476
  139.9 5.5 %reduce-scatter.2.cloned.1.call-done = f32[24,768]{1,0:T(8,128)} async-done(((f32[192,768]{1,0:T(8,128)}), f32[24,768]{1,0:T(8,128)}) %reduce-scatter.2.cloned.1.call-update) | async-done | bytes 73744 | tf_op jit(solution)/shard_map/reduce_scatter | solution.py:418
  (89 shorter events, 17.3 us)
Async XLA Ops:
  7.2 11.6 %copy-start = (bf16[256,1,768]{2,0,1:T(8,128)(2,1)S(1)}, bf16[256,1,768]{2,0,1:T(8,128)(2,1)}, u32[]{:S(2)}) copy-start(bf16[256,1,768]{2,0,1:T(8,128)(2,1)} %param.7) | copy-start | bytes 1179652
  7.2 27.8 %copy-start.1 = (bf16[256,1,768]{2,0,1:T(8,128)(2,1)S(1)}, bf16[256,1,768]{2,0,1:T(8,128)(2,1)}, u32[]{:S(2)}) copy-start(bf16[256,1,768]{2,0,1:T(8,128)(2,1)} %param.13) | copy-start | bytes 1179652
  9.6 26.9 %copy-start.32 = (f32[768]{0:T(1024)S(1)}, f32[768]{0:T(1024)}, u32[]{:S(2)}) copy-start(f32[768]{0:T(1024)} %param.8) | copy-start | bytes 9220
  9.6 30.4 %copy-start.31 = (bf16[24,768]{1,0:T(8,128)(2,1)S(1)}, bf16[24,768]{1,0:T(8,128)(2,1)}, u32[]{:S(2)}) copy-start(bf16[24,768]{1,0:T(8,128)(2,1)} %param.12) | copy-start | bytes 110596
  10.4 23.9 %all-to-all-start = ((bf16[16,24,576]{2,1,0:T(8,128)(2,1)}), bf16[16,24,576]{2,1,0:T(8,128)(2,1)S(1)}, u32[]{:S(2)}, u32[]{:S(2)}) async-start(bf16[16,24,576]{2,1,0:T(8,128)(2,1)} %shard_map.126), calls=%async_computation | async-start | bytes 983040 | tf_op jit(solution)/shard_map/all_to_all | solution.py:393
  18.8 17.7 %collective-permute-start.3 = (bf16[256,768]{1,0:T(8,128)(2,1)S(1)}, bf16[256,768]{1,0:T(8,128)(2,1)S(1)}, u32[]{:S(2)}, u32[]{:S(2)}) collective-permute-start(bf16[256,768]{1,0:T(8,128)(2,1)S(1)} %bitcast.15), channel_id=1, source_target_pairs={{0,8},{8,0},{16,24},{24,16},{1,9},{9,1},{17,25},{25,17},{2,10},{10... | collective-permute-start | bytes 1179656 | tf_op jit(solution)/shard_map/ppermute | solution.py:166
  20.8 17.9 %collective-permute-start.4 = (bf16[256,768]{1,0:T(8,128)(2,1)S(1)}, bf16[256,768]{1,0:T(8,128)(2,1)S(1)}, u32[]{:S(2)}, u32[]{:S(2)}) collective-permute-start(bf16[256,768]{1,0:T(8,128)(2,1)S(1)} %bitcast.16), channel_id=1, source_target_pairs={{0,16},{8,24},{16,0},{24,8},{1,17},{9,25},{17,1},{25,9},{2,18},{10... | collective-permute-start | bytes 1179656 | tf_op jit(solution)/shard_map/ppermute | solution.py:166
  34.4 20.5 %collective-permute-start.6 = (bf16[16,24,576]{2,1,0:T(8,128)(2,1)S(1)}, bf16[16,24,576]{2,1,0:T(8,128)(2,1)S(1)}, u32[]{:S(2)}, u32[]{:S(2)}) collective-permute-start(bf16[16,24,576]{2,1,0:T(8,128)(2,1)S(1)} %all-to-all-done.refs_6_), channel_id=1, source_target_pairs={{0,1},{1,0},{2,3},{3,2},{4,5},{5,4},{6,7},{7,6},{8,9},{9,8},{10,11... | collective-permute-start | bytes 1327112 | tf_op jit(solution)/shard_map/ppermute | solution.py:166
  34.4 19.8 %collective-permute-start.5 = (bf16[256,768]{1,0:T(8,128)(2,1)S(1)}, bf16[256,768]{1,0:T(8,128)(2,1)S(1)}, u32[]{:S(2)}, u32[]{:S(2)}) collective-permute-start(bf16[256,768]{1,0:T(8,128)(2,1)S(1)} %bitcast.17), channel_id=1, source_target_pairs={{0,24},{8,16},{16,8},{24,0},{1,25},{9,17},{17,9},{25,1},{2,26},{10... | collective-permute-start | bytes 1179656 | tf_op jit(solution)/shard_map/ppermute | solution.py:166
  34.9 38.4 %collective-permute-start = (bf16[256,768]{1,0:T(8,128)(2,1)S(1)}, bf16[256,768]{1,0:T(8,128)(2,1)}, u32[]{:S(2)}, u32[]{:S(2)}) collective-permute-start(bf16[256,768]{1,0:T(8,128)(2,1)S(1)} %bitcast.19), channel_id=1, source_target_pairs={{0,8},{8,0},{16,24},{24,16},{1,9},{9,1},{17,25},{25,17},{2,10},{10... | collective-permute-start | bytes 1179656 | tf_op jit(solution)/shard_map/ppermute | solution.py:166
  37.2 36.2 %collective-permute-start.1 = (bf16[256,768]{1,0:T(8,128)(2,1)S(1)}, bf16[256,768]{1,0:T(8,128)(2,1)S(1)}, u32[]{:S(2)}, u32[]{:S(2)}) collective-permute-start(bf16[256,768]{1,0:T(8,128)(2,1)S(1)} %bitcast.20), channel_id=1, source_target_pairs={{0,16},{8,24},{16,0},{24,8},{1,17},{9,25},{17,1},{25,9},{2,18},{10... | collective-permute-start | bytes 1179656 | tf_op jit(solution)/shard_map/ppermute | solution.py:166
  39.4 34.0 %collective-permute-start.2 = (bf16[256,768]{1,0:T(8,128)(2,1)S(1)}, bf16[256,768]{1,0:T(8,128)(2,1)S(1)}, u32[]{:S(2)}, u32[]{:S(2)}) collective-permute-start(bf16[256,768]{1,0:T(8,128)(2,1)S(1)} %bitcast.21), channel_id=1, source_target_pairs={{0,24},{8,16},{16,8},{24,0},{1,25},{9,17},{17,9},{25,1},{2,26},{10... | collective-permute-start | bytes 1179656 | tf_op jit(solution)/shard_map/ppermute | solution.py:166
  55.7 1.0 copy-start.12
  77.2 21.0 %collective-permute-start.7 = (bf16[256,768]{1,0:T(8,128)(2,1)}, bf16[256,768]{1,0:T(8,128)(2,1)S(1)}, u32[]{:S(2)}, u32[]{:S(2)}) collective-permute-start(bf16[256,768]{1,0:T(8,128)(2,1)} %get-tuple-element.56), channel_id=1, source_target_pairs={{0,8},{8,0},{16,24},{24,16},{1,9},{9,1},{17,25},{25,17},{2,10},{10... | collective-permute-start | bytes 1179656 | tf_op jit(solution)/shard_map/ppermute | solution.py:166
  78.7 19.7 %collective-permute-start.8 = (bf16[256,768]{1,0:T(8,128)(2,1)}, bf16[256,768]{1,0:T(8,128)(2,1)S(1)}, u32[]{:S(2)}, u32[]{:S(2)}) collective-permute-start(bf16[256,768]{1,0:T(8,128)(2,1)} %get-tuple-element.57), channel_id=1, source_target_pairs={{0,16},{8,24},{16,0},{24,8},{1,17},{9,25},{17,1},{25,9},{2,18},{10... | collective-permute-start | bytes 1179656 | tf_op jit(solution)/shard_map/ppermute | solution.py:166
  80.2 18.3 %collective-permute-start.9 = (bf16[256,768]{1,0:T(8,128)(2,1)}, bf16[256,768]{1,0:T(8,128)(2,1)S(1)}, u32[]{:S(2)}, u32[]{:S(2)}) collective-permute-start(bf16[256,768]{1,0:T(8,128)(2,1)} %get-tuple-element.58), channel_id=1, source_target_pairs={{0,24},{8,16},{16,8},{24,0},{1,25},{9,17},{17,9},{25,1},{2,26},{10... | collective-permute-start | bytes 1179656 | tf_op jit(solution)/shard_map/ppermute | solution.py:166
  81.7 1.0 copy-start.7
  82.7 1.0 copy-start.20
  83.7 1.0 copy-start.22
  84.8 1.0 copy-start.24
  86.8 11.6 %copy-start.3 = (bf16[768,576]{1,0:T(8,128)(2,1)S(1)}, bf16[768,576]{1,0:T(8,128)(2,1)}, u32[]{:S(2)}) copy-start(bf16[768,576]{1,0:T(8,128)(2,1)} %copy-done.2) | copy-start | bytes 2654212
  98.2 2.3 %copy-start.27 = (bf16[256,768]{1,0:T(8,128)(2,1)}, bf16[256,768]{1,0:T(8,128)(2,1)S(1)}, u32[]{:S(2)}) copy-start(bf16[256,768]{1,0:T(8,128)(2,1)S(1)} %collective-permute-done.7) | copy-start | bytes 1179652
  98.4 2.1 %copy-start.29 = (bf16[256,768]{1,0:T(8,128)(2,1)}, bf16[256,768]{1,0:T(8,128)(2,1)S(1)}, u32[]{:S(2)}) copy-start(bf16[256,768]{1,0:T(8,128)(2,1)S(1)} %collective-permute-done.8) | copy-start | bytes 1179652
  98.4 2.1 %copy-start.30 = (bf16[256,768]{1,0:T(8,128)(2,1)}, bf16[256,768]{1,0:T(8,128)(2,1)S(1)}, u32[]{:S(2)}) copy-start(bf16[256,768]{1,0:T(8,128)(2,1)S(1)} %collective-permute-done.9) | copy-start | bytes 1179652
  100.5 1.9 %collective-permute-start.10 = (bf16[16,24,640]{2,1,0:T(8,128)(2,1)S(1)}, bf16[16,24,640]{2,1,0:T(8,128)(2,1)S(1)}, u32[]{:S(2)}, u32[]{:S(2)}) collective-permute-start(bf16[16,24,640]{2,1,0:T(8,128)(2,1)S(1)} %get-tuple-element.68), channel_id=1, source_target_pairs={{0,1},{1,0},{2,3},{3,2},{4,5},{5,4},{6,7},{7,6},{8,9},{9,8},{10,11... | collective-permute-start | bytes 1474568 | tf_op jit(solution)/shard_map/ppermute | solution.py:166
  103.3 32.0 %copy-start.33 = (f32[768]{0:T(1024)S(1)}, f32[768]{0:T(1024)}, u32[]{:S(2)}) copy-start(f32[768]{0:T(1024)} %param.8) | copy-start | bytes 9220
  103.3 31.2 %all-to-all-start.1 = ((bf16[16,24,640]{2,1,0:T(8,128)(2,1)}), bf16[16,24,640]{2,1,0:T(8,128)(2,1)S(1)}, u32[]{:S(2)}, u32[]{:S(2)}) async-start(bf16[16,24,640]{2,1,0:T(8,128)(2,1)} %add_convert_fusion), calls=%async_computation.1 | async-start | bytes 983040 | tf_op jit(solution)/shard_map/all_to_all | solution.py:452
  108.8 36.6 %reduce-scatter.2.cloned.1.call-start = ((), (), s32[]{:S(2)}) async-start(), calls=%async_computation.3 | async-start | bytes 663552 | tf_op jit(solution)/shard_map/reduce_scatter | solution.py:418
  109.0 17.2 %collective-permute-start.11 = (bf16[256,768]{1,0:T(8,128)(2,1)S(1)}, bf16[256,768]{1,0:T(8,128)(2,1)}, u32[]{:S(2)}, u32[]{:S(2)}) collective-permute-start(bf16[256,768]{1,0:T(8,128)(2,1)S(1)} %get-tuple-element.76), channel_id=1, source_target_pairs={{0,8},{8,0},{16,24},{24,16},{1,9},{9,1},{17,25},{25,17},{2,10},{10... | collective-permute-start | bytes 1179656 | tf_op jit(solution)/shard_map/ppermute | solution.py:166
  111.0 15.4 %collective-permute-start.12 = (bf16[256,768]{1,0:T(8,128)(2,1)S(1)}, bf16[256,768]{1,0:T(8,128)(2,1)}, u32[]{:S(2)}, u32[]{:S(2)}) collective-permute-start(bf16[256,768]{1,0:T(8,128)(2,1)S(1)} %get-tuple-element.77), channel_id=1, source_target_pairs={{0,16},{8,24},{16,0},{24,8},{1,17},{9,25},{17,1},{25,9},{2,18},{10... | collective-permute-start | bytes 1179656 | tf_op jit(solution)/shard_map/ppermute | solution.py:166
  112.4 22.0 %collective-permute-start.13 = (bf16[256,768]{1,0:T(8,128)(2,1)S(1)}, bf16[256,768]{1,0:T(8,128)(2,1)}, u32[]{:S(2)}, u32[]{:S(2)}) collective-permute-start(bf16[256,768]{1,0:T(8,128)(2,1)S(1)} %get-tuple-element.78), channel_id=1, source_target_pairs={{0,24},{8,16},{16,8},{24,0},{1,25},{9,17},{17,9},{25,1},{2,26},{10... | collective-permute-start | bytes 1179656 | tf_op jit(solution)/shard_map/ppermute | solution.py:166
  126.1 11.3 %copy-start.28 = (bf16[256,768]{1,0:T(8,128)(2,1)S(1)}, bf16[256,768]{1,0:T(8,128)(2,1)}, u32[]{:S(2)}) copy-start(bf16[256,768]{1,0:T(8,128)(2,1)} %copy-done.27) | copy-start | bytes 1179652
  (19 other events, 16.1 us)
Sparse Core Ops, SparseCore 0:
  112.9 32.4 reduce-scatter.1
